TPU v7x, 256 devices: a whole 4x4x8 slice. The times are simulated.
256 devices in a mesh: wa: 8 (over z_lo, x), ha: 32 (over y, z_hi, core).
Axes of the slice: x: 4, y: 4, z: 8 (z_hi: 4, z_lo: 2; z = z_hi * 2 + z_lo), core: 2. Of those that a mesh axis runs over, the one named last changes fastest.
Arguments:
- tokens: float32 [256, 5376], P('ha', 'wa'), may hold values from -6 to 6
- grad_out: float32 [256, 5376], P('ha', 'wa'), may hold values from -1.5 to 1.5
- gate_weight: float32 [5376, 10752], P('wa', 'ha'), may hold values from -0.078125 to 0.078125
- up_weight: float32 [5376, 10752], P('wa', 'ha'), may hold values from -0.078125 to 0.078125
- down_weight: float32 [10752, 5376], P('ha', 'wa'), may hold values from -0.0625 to 0.0625
Outputs:
- grad_tokens: float32 [256, 5376], P('ha', 'wa')
- grad_gate: float32 [5376, 10752], P('wa', 'ha')
- grad_up: float32 [5376, 10752], P('wa', 'ha')
- grad_down: float32 [10752, 5376], P('ha', 'wa')
All inputs are finite; a program needn't handle non-finite values.
Results may differ from a plain program's by a relative error of at most 0.00018.
Values sent between devices are 32-bit elements; how exact they have to be, the bound alone decides.
A program may use at most 64 MiB of HBM per device.

v0:
```python
import jax
import jax.numpy as jnp
from jax import lax
from jax.sharding import PartitionSpec as P


def side_by_side(arrays, axis, dim, along):
    ends, at = ([], 0)
    for a in arrays[:-1]:
        at += a.shape[along]
        ends.append(at)
    both = jnp.concatenate(arrays, axis=along)
    return tuple(jnp.split(lax.all_gather(both, axis, axis=dim, tiled=True), ends, axis=along))


def in_blocks(array, dim, count):
    before, after = (array.shape[:dim], array.shape[dim + 1 :])
    return jnp.moveaxis(array.reshape(*before, count, -1, *after), dim, 0)


def summed_on_arrival(array, axis, dim):
    count = lax.axis_size(axis)
    blocks = lax.all_to_all(in_blocks(array, dim, count), axis, 0, 0, tiled=True)
    return jnp.sum(blocks, axis=0)


def sent_to_all(array, axis):
    copies = jnp.broadcast_to(array, (lax.axis_size(axis), *array.shape))
    return lax.all_to_all(copies, axis, split_axis=0, concat_axis=0, tiled=True)


def in_order(blocks, dim):
    blocks = jnp.moveaxis(blocks, 0, dim)
    lengths = blocks.shape
    return blocks.reshape(*lengths[:dim], lengths[dim] * lengths[dim + 1], *lengths[dim + 2 :])


def gathered_copies(array, axis, dim):
    blocks = sent_to_all(array, axis)
    return in_order(blocks, dim)


def side_by_side_2(arrays, axis, dim, along):
    both = jnp.concatenate(arrays, axis=along)
    result, at, finished = (gathered_copies(both, axis, dim), 0, [])
    for a in arrays:
        finished.append(lax.slice_in_dim(result, at, at + a.shape[along], axis=along))
        at += a.shape[along]
    return tuple(finished)


def contract(left, right, left_dim, right_dim):
    return lax.dot_general(
        left,
        right,
        (((left_dim,), (right_dim,)), ((), ())),
        preferred_element_type=jnp.float32,
        precision=lax.Precision.HIGHEST,
    )


def derivs(gate, up, grad_hidden):
    sig = 1.0 / (1.0 + jnp.exp(-gate))
    hidden = gate * sig * up
    grad_up_act = grad_hidden * gate * sig
    grad_gate_act = grad_hidden * up * sig * (1.0 + gate * (1.0 - sig))
    return (hidden, grad_gate_act, grad_up_act)


def per_device(tokens, grad_out, gate_weight, up_weight, down_weight):
    inputs, upstream = side_by_side((tokens, grad_out), "ha", 0, 1)
    width = gate_weight.shape[1]
    gate = contract(inputs, gate_weight, 1, 0)
    up = contract(inputs, up_weight, 1, 0)
    grad_hidden = contract(upstream, down_weight, 1, 1)
    shares = summed_on_arrival(jnp.concatenate([gate, up, grad_hidden], axis=1), "wa", 0)
    local_vals = derivs(shares[:, :width], shares[:, width : 2 * width], shares[:, 2 * width :])
    hidden, grad_gate_act, grad_up_act = side_by_side_2(
        (local_vals[0], local_vals[1], local_vals[2]), "wa", 0, 1
    )
    grad_down = contract(hidden, upstream, 0, 0)
    grad_gate = contract(inputs, grad_gate_act, 0, 0)
    grad_up = contract(inputs, grad_up_act, 0, 0)
    grad_tokens = summed_on_arrival(
        contract(grad_gate_act, gate_weight, 1, 1) + contract(grad_up_act, up_weight, 1, 1), "ha", 0
    )
    return (grad_tokens, grad_gate, grad_up, grad_down)


def solution(mesh):
    placed = (P("ha", "wa"), P("ha", "wa"), P("wa", "ha"), P("wa", "ha"), P("ha", "wa"))
    return jax.shard_map(
        per_device,
        mesh=mesh,
        in_specs=placed,
        out_specs=(P("ha", "wa"), P("wa", "ha"), P("wa", "ha"), P("ha", "wa")),
        check_vma=False,
    )
```

profile of v0, /device:TPU:1, one launch (start us, length us, event | category | flops | bytes accessed | tf_op | source)
XLA Modules:
  0.0 162.7 jit_solution(16663557393100656889)
XLA Ops:
  7.2 0.0 copy-start
  7.2 0.0 all-gather.2.cloned.1.call-start
  7.2 1.5 pad_maximum_fusion.2
  8.8 0.0 all-gather.2.cloned.1.call-update
  8.8 59.5 %all-gather.2.cloned.1.call-done = f32[256,1344]{1,0:T(8,128)} async-done(((f32[8,1344]{1,0:T(8,128)}), f32[256,1344]{1,0:T(8,128)}) %all-gather.2.cloned.1.call-update) | async-done | bytes 1376272 | tf_op jit(solution)/shard_map/all_gather | solution.py:13
  68.3 0.0 copy-start.1
  68.3 3.5 %fusion.8 = f32[256,336]{0,1:T(8,128)S(1)} fusion(f32[672,336]{1,0:T(8,128)} %param.8, f32[256,1344]{1,0:T(8,128)} %all-gather.2.cloned.1.call-done), kind=kOutput, calls=%fused_computation.10 | convolution fusion | flops 693633024 | bytes 2162688 | tf_op jit(solution)/shard_map/dot_general | solution.py:53
  71.8 0.0 copy-done.1
  71.8 2.3 %fusion.2 = f32[256,336]{0,1:T(8,128)S(1)} fusion(f32[336,672]{1,0:T(8,128)} %param.9, f32[256,1344]{1,0:T(8,128)S(1)} %copy-done.1), kind=kOutput, calls=%fused_computation.4 | convolution fusion | flops 693633024 | bytes 2033664 | tf_op jit(solution)/shard_map/dot_general | solution.py:53
  74.2 0.0 copy-done
  74.2 2.0 %fusion.10 = f32[256,336]{0,1:T(8,128)S(1)} fusion(f32[672,336]{1,0:T(8,128)S(1)} %copy-done, f32[256,1344]{1,0:T(8,128)S(1)} %copy-done.1), kind=kOutput, calls=%fused_computation.12 | convolution fusion | flops 693633024 | bytes 2162688 | tf_op jit(solution)/shard_map/dot_general | solution.py:53
  76.1 1.0 pad_maximum_fusion
  77.2 1.5 copy.9
  78.7 18.2 %all_to_all.15 = f32[8,32,1008]{2,1,0:T(8,128)} all-to-all(f32[8,32,1008]{2,1,0:T(8,128)S(1)} %bitcast.13), channel_id=1, replica_groups=mesh['wa'=8,'ha'=32] {'wa'}, dimensions={0} | all-to-all | bytes 2064384 | tf_op jit(solution)/shard_map/all_to_all | solution.py:23
  96.9 1.3 reduce_sum.18
  98.2 0.1 multiply_multiply_fusion.1
  98.3 0.1 pad_maximum_fusion.1
  98.4 0.1 broadcast_in_dim.3
  98.5 18.2 %all_to_all.16 = f32[8,32,1008]{2,1,0:T(8,128)S(1)} all-to-all(f32[8,32,1008]{2,1,0:T(8,128)S(1)} %broadcast_in_dim.3), channel_id=1, replica_groups=mesh['wa'=8,'ha'=32] {'wa'}, dimensions={0} | all-to-all | bytes 2064384 | tf_op jit(solution)/shard_map/all_to_all | solution.py:29
  116.7 0.0 copy-start.2
  116.7 1.3 fusion.16
  118.1 0.0 copy-done.2
  118.1 2.2 %convolution_add_fusion = f32[256,672]{0,1:T(8,128)} fusion(f32[256,672]{0,1:T(8,128)S(1)} %fusion.16, f32[672,336]{1,0:T(8,128)S(1)} %copy-done.2, f32[256,1008]{1,0:T(8,128)S(1)} %bitcast.9), kind=kOutput, calls=%fused_computation | convolution fusion | flops 693805056 | bytes 2801664 | tf_op jit(solution)/shard_map/dot_general | solution.py:53
  120.3 2.3 %copy.10 = f32[256,672]{1,0:T(8,128)} copy(f32[256,672]{0,1:T(8,128)} %convolution_add_fusion) | data formatting | bytes 1376256 | tf_op jit(solution)/shard_map/add | solution.py:85
  122.5 8.3 %all-to-all-start.2 = ((f32[32,8,672]{2,1,0:T(8,128)}), f32[32,8,672]{2,1,0:T(8,128)}, u32[]{:S(2)}, u32[]{:S(2)}) async-start(f32[32,8,672]{2,1,0:T(8,128)} %bitcast.14), calls=%async_computation.2 | async-start | bytes 1572864 | tf_op jit(solution)/shard_map/all_to_all | solution.py:23
  130.9 2.5 %fusion.6 = f32[672,336]{1,0:T(8,128)} fusion(f32[256,1344]{1,0:T(8,128)S(1)} %copy-done.1, f32[256,1008]{1,0:T(8,128)S(1)} %bitcast.10), kind=kOutput, calls=%fused_computation.8 | convolution fusion | flops 693633024 | bytes 2082816 | tf_op jit(solution)/shard_map/dot_general | solution.py:53
  133.4 2.6 %fusion.4 = f32[672,336]{1,0:T(8,128)} fusion(f32[256,1344]{1,0:T(8,128)S(1)} %copy-done.1, f32[256,1008]{1,0:T(8,128)S(1)} %bitcast.11), kind=kOutput, calls=%fused_computation.6 | convolution fusion | flops 693633024 | bytes 2082816 | tf_op jit(solution)/shard_map/dot_general | solution.py:53
  136.0 2.2 %fusion = f32[336,672]{1,0:T(8,128)} fusion(f32[256,1344]{1,0:T(8,128)S(1)} %copy-done.1, f32[256,1008]{1,0:T(8,128)S(1)} %bitcast.12), kind=kOutput, calls=%fused_computation.2 | convolution fusion | flops 693633024 | bytes 2082816 | tf_op jit(solution)/shard_map/dot_general | solution.py:53
  138.2 15.8 %all-to-all-done.2 = f32[32,8,672]{2,1,0:T(8,128)} async-done(((f32[32,8,672]{2,1,0:T(8,128)}), f32[32,8,672]{2,1,0:T(8,128)}, u32[]{:S(2)}, u32[]{:S(2)}) %all-to-all-start.2) | async-done | bytes 688160 | tf_op jit(solution)/shard_map/all_to_all | solution.py:23
  154.0 1.8 %reduce_sum.19 = f32[8,672]{1,0:T(8,128)} reduce(f32[32,8,672]{2,1,0:T(8,128)} %all-to-all-done.2, f32[]{:T(128)} %constant.0.clone.1), dimensions={0}, to_apply=%region_1.0 | reduce | flops 166656 | bytes 709636 | tf_op jit(solution)/shard_map/reduce_sum | solution.py:24
Async XLA Ops:
  7.2 67.0 %copy-start = (f32[672,336]{1,0:T(8,128)S(1)}, f32[672,336]{1,0:T(8,128)}, u32[]{:S(2)}) copy-start(f32[672,336]{1,0:T(8,128)} %param.7) | copy-start | bytes 2709508
  7.2 61.1 %all-gather.2.cloned.1.call-start = ((), (), s32[]{:S(2)}) async-start(), calls=%async_computation.3 | async-start | bytes 1486848 | tf_op jit(solution)/shard_map/all_gather | solution.py:13
  68.3 3.5 %copy-start.1 = (f32[256,1344]{1,0:T(8,128)S(1)}, f32[256,1344]{1,0:T(8,128)}, u32[]{:S(2)}) copy-start(f32[256,1344]{1,0:T(8,128)} %all-gather.2.cloned.1.call-done) | copy-start | bytes 4128772
  116.7 1.4 copy-start.2
  122.5 31.5 %all-to-all-start.2 = ((f32[32,8,672]{2,1,0:T(8,128)}), f32[32,8,672]{2,1,0:T(8,128)}, u32[]{:S(2)}, u32[]{:S(2)}) async-start(f32[32,8,672]{2,1,0:T(8,128)} %bitcast.14), calls=%async_computation.2 | async-start | bytes 1572864 | tf_op jit(solution)/shard_map/all_to_all | solution.py:23
Sparse Core Ops, SparseCore 0:
  11.2 57.0 all-gather.1
where the time goes:
time: 163 us
  waiting for transfers between devices  75.4 us (46%)
  blocking collectives  36.4 us (22%)
  matrix products  18.7 us (11%)
  between operations  14.1 us (9%)
  starting transfers between devices  8.34 us (5%)
  other arithmetic  5.84 us (4%)
  local copies, waits for them, and re-layouts  3.93 us (2%)
    all_gather x1, waiting for transfers between devices, side_by_side(): lax.all_gather(both, axis, axis=dim, tiled=True)  59.5 us
    dot_general x8, matrix products, contract(): lax.dot_general(left, right, (((left_dim,), (right_dim,)), ((), ())), pre...  18.7 us
    all_to_all x1, blocking collectives, sent_to_all(): return lax.all_to_all(copies, axis, split_axis=0, concat_axis=0, tiled=True)  18.2 us
    all_to_all x1, blocking collectives, summed_on_arrival(): lax.all_to_all(in_blocks(array, dim, count), axis, 0, 0, tiled=True)  18.2 us
    all_to_all x1, waiting for transfers between devices, summed_on_arrival(): lax.all_to_all(in_blocks(array, dim, count), axis, 0, 0, tiled=True)  15.8 us
    all_to_all x1, starting transfers between devices, summed_on_arrival(): lax.all_to_all(in_blocks(array, dim, count), axis, 0, 0, tiled=True)  8.3 us
  transfers between devices with their start and end apart: 2, of which 2 were waited for; matrix products, arithmetic and copies ran while one was open for 5% of the time, Pallas kernels for 0%

commit v1 on v0

v1 whole, which is shorter than its diff:
```python
import jax
import jax.numpy as jnp
from jax import lax
from jax.experimental import pallas as pl
from jax.experimental.pallas import tpu as pltpu
from jax.sharding import PartitionSpec as P

MESH = pl.DeviceIdType.MESH
F32, BF16 = jnp.float32, jnp.bfloat16
DL, FL = 672, 336
DP, FP = 768, 384
XW, AW = 1408, 1024
STEPS = (0, 1, 3, 2)


def split(v):
    hi = v.astype(BF16)
    return hi, (v - hi.astype(F32)).astype(BF16)


def dot(a, b, ad, bd):
    return lax.dot_general(a, b, (((ad,), (bd,)), ((), ())), preferred_element_type=F32)


def pack3(a, b, c):
    rows = a.shape[0]
    return jnp.concatenate([a[:, :FL], b[:, :FL], c[:, :FL], jnp.zeros((rows, AW - 3 * FL), F32)], axis=1)


def unpack3(p):
    pad = jnp.zeros((p.shape[0], FP - FL), F32)
    return [jnp.concatenate([p[:, i * FL : (i + 1) * FL], pad], axis=1) for i in range(3)]


def derivs(gate, up, grad_hidden):
    sig = 1.0 / (1.0 + jnp.exp(-gate))
    hidden = gate * sig * up
    grad_up_act = grad_hidden * gate * sig
    grad_gate_act = grad_hidden * up * sig * (1.0 + gate * (1.0 - sig))
    return grad_gate_act, grad_up_act, hidden


def kernel(
    tok, gro, wg_hbm, wu_hbm, wd_hbm,
    o_tok, o_g, o_u, o_d,
    wg, wu, wd, wgu_h, wgu_l, wd_h, wd_l,
    x, xt_h, xt_l, xg_h, xg_l,
    part, part_in, acts, a_h, a_l,
    gb, gb_in, q, q_in, r, r_in, og, ou, od,
    w_sem, az_s, az_r, ay_s, ay_r, as_s, as_r, fs_s, fs_r,
    b_s, b_r, c_s, c_r, d1_s, d1_r, d2_s, d2_r, d3_s, d3_r, o_sem,
):
    wa, ha = lax.axis_index("wa"), lax.axis_index("ha")
    y, zh, c = ha // 8, (ha // 2) % 4, ha % 2

    def dev(w, yy, zz, cc):
        return (w, yy * 8 + zz * 2 + cc)

    sibling = dev(wa, y, zh, 1 - c)
    z_peers = [dev(wa, y, (zh + i) % 4, c) for i in (1, 2, 3)]
    y_peers = [dev(wa, (y + s) % 4, zh, c) for s in STEPS[1:]]
    w_peers = [dev((wa + i) % 8, y, zh, c) for i in range(1, 8)]

    loads = [
        pltpu.make_async_copy(wg_hbm, wg, w_sem.at[0]),
        pltpu.make_async_copy(wu_hbm, wu, w_sem.at[1]),
        pltpu.make_async_copy(wd_hbm, wd, w_sem.at[2]),
    ]
    for cp in loads:
        cp.start()

    barrier = pltpu.get_barrier_semaphore()
    for d in [sibling, *z_peers, *y_peers, *w_peers]:
        pl.semaphore_signal(barrier, inc=1, device_id=d, device_id_type=MESH)
    t, g = tok[...], gro[...]
    x[y, c, zh] = jnp.concatenate([t[:, :640], g[:, :640], t[:, 640:], g[:, 640:], jnp.zeros((8, 64), F32)], axis=1)
    pl.semaphore_wait(barrier, 14)

    sends = []

    def send(src, dst, ss, rs, d):
        cp = pltpu.make_async_remote_copy(src_ref=src, dst_ref=dst, send_sem=ss, recv_sem=rs, device_id=d, device_id_type=MESH)
        cp.start()
        sends.append(cp)

    def arrived(ref, sem):
        pltpu.make_async_copy(ref, ref, sem).wait()

    own = x.at[y, c, zh]
    for i in range(3):
        send(own, own, az_s.at[i], az_r.at[i], z_peers[i])
    for k in range(3):
        send(own, own, ay_s.at[0, k], ay_r.at[k, 0], y_peers[k])
    send(own, own, as_s.at[0], as_r.at[0], sibling)

    wgu_h[DL:, :] = jnp.zeros((DP - DL, DP), BF16)
    wgu_l[DL:, :] = jnp.zeros((DP - DL, DP), BF16)
    wd_h[FL:, :] = jnp.zeros((FP - FL, DP), BF16)
    wd_l[FL:, :] = jnp.zeros((FP - FL, DP), BF16)
    loads[0].wait()
    loads[1].wait()

    @pl.loop(0, 7)
    def _(i):
        rows = pl.ds(pl.multiple_of(i * 96, 96), 96)
        pad = jnp.zeros((96, FP - FL), F32)
        hi, lo = split(jnp.concatenate([wg[rows, :], pad], axis=1))
        wgu_h[rows, :FP], wgu_l[rows, :FP] = hi, lo
        hi, lo = split(jnp.concatenate([wu[rows, :], pad], axis=1))
        wgu_h[rows, FP:], wgu_l[rows, FP:] = hi, lo

    loads[2].wait()

    @pl.loop(0, 7)
    def _(i):
        rows = pl.ds(pl.multiple_of(i * 48, 48), 48)
        hi, lo = split(jnp.concatenate([wd[rows, :], jnp.zeros((48, DP - DL), F32)], axis=1))
        wd_h[rows, :], wd_l[rows, :] = hi, lo

    for i in range(3):
        block = x.at[y, c, (zh - i - 1 + 4) % 4]
        arrived(block, az_r.at[i])
        for k in range(3):
            send(block, block, ay_s.at[i + 1, k], ay_r.at[k, i + 1], y_peers[k])
        send(block, block, as_s.at[i + 1], as_r.at[i + 1], sibling)

    def source_y(k):
        return (y + 4 - STEPS[k]) % 4

    def forward(k):
        yy = source_y(k)
        for i in range(4):
            arrived(x.at[yy, c, (zh - i + 4) % 4], ay_r.at[k - 1, i])
        send(x.at[yy, c], x.at[yy, c], fs_s.at[k - 1], fs_r.at[k - 1], sibling)

    lane = lax.broadcasted_iota(jnp.int32, (64, 128), 1)

    def project(k):
        yy = source_y(k)
        if k == 0:
            for i in range(4):
                arrived(x.at[yy, 1 - c, (zh - i + 4) % 4], as_r.at[i])
        else:
            arrived(x.at[yy, 1 - c], fs_r.at[k - 1])
        rows = pl.ds(pl.multiple_of(yy * 64, 64), 64)
        v = x[yy].reshape(64, XW)
        mixed = v[:, 1280:]
        th, tl = split(jnp.concatenate([v[:, :640], jnp.where(lane < 32, mixed, 0.0)], axis=1))
        gh, gl = split(jnp.concatenate([v[:, 640:1280], jnp.where(lane < 32, pltpu.roll(mixed, 96, 1), 0.0)], axis=1))
        xt_h[rows, :], xt_l[rows, :] = th, tl
        xg_h[rows, :], xg_l[rows, :] = gh, gl
        both = jnp.concatenate([th, tl], axis=0)
        gu = dot(both, wgu_h[...], 1, 0)
        gu = gu[:64] + gu[64:] + dot(th, wgu_l[...], 1, 0)
        both = jnp.concatenate([gh, gl], axis=0)
        hid = dot(both, wd_h[...], 1, 1)
        hid = hid[:64] + hid[64:] + dot(gh, wd_l[...], 1, 1)
        part[k] = pack3(gu[:, :FP], gu[:, FP:], hid).reshape(8, 8, AW)
        for i in range(7):
            send(part.at[k, (wa + i + 1) % 8], part_in.at[k, i], b_s.at[k, i], b_r.at[k, i], w_peers[i])

    def activate(k):
        yy = source_y(k)
        total = part[k, wa]
        for i in range(7):
            arrived(part_in.at[k, i], b_r.at[k, i])
            total = total + part_in[k, i]
        gate, up, gh = unpack3(total)
        acts[yy, wa] = pack3(*derivs(gate, up, gh))
        mine = acts.at[yy, wa]
        for i in range(7):
            send(mine, mine, c_s.at[k, i], c_r.at[k, i], w_peers[i])

    def back(k):
        yy = source_y(k)
        for i in range(7):
            arrived(acts.at[yy, (wa - i - 1 + 8) % 8], c_r.at[k, i])
        rows = pl.ds(pl.multiple_of(yy * 64, 64), 64)
        gga, gua, hid = unpack3(acts[yy].reshape(64, AW))
        ah, al = split(jnp.concatenate([gga, gua], axis=1))
        hh, hl = split(hid)
        a_h[rows, :DP], a_l[rows, :DP] = ah, al
        a_h[rows, DP:], a_l[rows, DP:] = hh, hl
        both = jnp.concatenate([ah, al], axis=0)
        gt = dot(both, wgu_h[...], 1, 1)
        gt = gt[:64] + gt[64:] + dot(ah, wgu_l[...], 1, 1)
        gb[k] = gt.reshape(2, 4, 8, DP)
        send(gb.at[k, 1 - c], gb_in.at[k], d1_s.at[k], d1_r.at[k], sibling)

    def home(k):
        arrived(gb_in.at[k], d1_r.at[k])
        q[k] = gb[k, c] + gb_in[k]
        if k:
            yy = source_y(k)
            send(q.at[k], q_in.at[k - 1], d2_s.at[k - 1], d2_r.at[k - 1], dev(wa, yy, zh, c))

    project(0)
    forward(1)
    forward(2)
    project(1)
    activate(0)
    project(2)
    forward(3)
    activate(1)
    project(3)
    back(0)
    activate(2)
    back(1)
    home(0)
    activate(3)
    back(2)
    home(1)
    back(3)
    home(2)

    stores = []

    def store(src, dst, i):
        cp = pltpu.make_async_copy(src, dst, o_sem.at[i])
        cp.start()
        stores.append(cp)

    def grad(lh, ll, rh, rl):
        return dot(lh, rh, 0, 0) + dot(lh, rl, 0, 0) + dot(ll, rh, 0, 0)

    home(3)
    gg = grad(xt_h[...], xt_l[...], a_h[:, :FP], a_l[:, :FP])
    og[...] = gg[:DL, :FL]
    store(og, o_g, 0)

    total = q[0]
    for k in range(3):
        arrived(q_in.at[k], d2_r.at[k])
        total = total + q_in[k]
    r[...] = total
    for i in range(3):
        send(r.at[(zh + i + 1) % 4], r_in.at[i], d3_s.at[i], d3_r.at[i], z_peers[i])

    gg = grad(xt_h[...], xt_l[...], a_h[:, FP:DP], a_l[:, FP:DP])
    ou[...] = gg[:DL, :FL]
    store(ou, o_u, 1)
    gg = grad(a_h[:, DP:], a_l[:, DP:], xg_h[...], xg_l[...])
    od[...] = gg[:FL, :DL]
    store(od, o_d, 2)

    total = r[zh]
    for i in range(3):
        arrived(r_in.at[i], d3_r.at[i])
        total = total + r_in[i]
    o_tok[...] = total[:, :DL]
    for cp in sends:
        cp.wait_send()
    for cp in stores:
        cp.wait()


def per_device(tokens, grad_out, gate_weight, up_weight, down_weight):
    vm, anym = pl.BlockSpec(memory_space=pltpu.VMEM), pl.BlockSpec(memory_space=pltpu.MemorySpace.HBM)
    dma = pltpu.SemaphoreType.DMA
    v = pltpu.VMEM
    return pl.pallas_call(
        kernel,
        out_shape=(
            jax.ShapeDtypeStruct((8, DL), F32),
            jax.ShapeDtypeStruct((DL, FL), F32),
            jax.ShapeDtypeStruct((DL, FL), F32),
            jax.ShapeDtypeStruct((FL, DL), F32),
        ),
        in_specs=[vm, vm, anym, anym, anym],
        out_specs=(vm, anym, anym, anym),
        scratch_shapes=[
            v((DL, FL), F32), v((DL, FL), F32), v((FL, DL), F32),
            v((DP, DP), BF16), v((DP, DP), BF16), v((FP, DP), BF16), v((FP, DP), BF16),
            v((4, 2, 4, 8, XW), F32),
            v((256, DP), BF16), v((256, DP), BF16), v((256, DP), BF16), v((256, DP), BF16),
            v((4, 8, 8, AW), F32), v((4, 7, 8, AW), F32), v((4, 8, 8, AW), F32),
            v((256, DP + FP), BF16), v((256, DP + FP), BF16),
            v((4, 2, 4, 8, DP), F32), v((4, 4, 8, DP), F32), v((4, 4, 8, DP), F32), v((3, 4, 8, DP), F32),
            v((4, 8, DP), F32), v((3, 8, DP), F32),
            v((DL, FL), F32), v((DL, FL), F32), v((FL, DL), F32),
            dma((3,)), dma((3,)), dma((3,)), dma((4, 3)), dma((3, 4)), dma((4,)), dma((4,)), dma((3,)), dma((3,)),
            dma((4, 7)), dma((4, 7)), dma((4, 7)), dma((4, 7)),
            dma((4,)), dma((4,)), dma((3,)), dma((3,)), dma((3,)), dma((3,)), dma((3,)),
        ],
        compiler_params=pltpu.CompilerParams(collective_id=0, has_side_effects=True, vmem_limit_bytes=40 * 2**20),
        name="feed_forward_backward",
    )(tokens, grad_out, gate_weight, up_weight, down_weight)


def solution(mesh):
    placed = (P("ha", "wa"), P("ha", "wa"), P("wa", "ha"), P("wa", "ha"), P("ha", "wa"))
    return jax.shard_map(
        per_device,
        mesh=mesh,
        in_specs=placed,
        out_specs=(P("ha", "wa"), P("wa", "ha"), P("wa", "ha"), P("ha", "wa")),
        check_vma=False,
    )
```

time: 163 us -> 70 us (0.43)
  waiting for transfers between devices: 75.4 us -> 0 us
  Pallas kernels: 0 us -> 60.2 us
  blocking collectives: 36.4 us -> 0 us
  matrix products: 18.7 us -> 0 us
  between operations: 14.1 us -> 0.65 us
  starting transfers between devices: 8.34 us -> 0 us
  other arithmetic: 5.84 us -> 0 us
  local copies, waits for them, and re-layouts: 3.93 us -> 8.61 us
    pallas_call x0 -> x1, Pallas kernels: none -> 60.2 us  [per_device(): pl.pallas_call(kernel, out_shape=(jax.ShapeDtypeStruct((8, DL), F32), jax...]
    all_gather x1 -> x0, waiting for transfers between devices: 59.5 us -> none  [side_by_side(): lax.all_gather(both, axis, axis=dim, tiled=True)]
    all_to_all x2 -> x0, blocking collectives: 36.4 us -> none  [the longest x1 18.2 us: sent_to_all(): return lax.all_to_all(copies, axis, split_axis=0, concat_axis=0, tiled=True)]
    dot_general x8 -> x0, matrix products: 18.7 us -> none  [contract(): lax.dot_general(left, right, (((left_dim,), (right_dim,)), ((), ())), pre...]
    all_to_all x1 -> x0, waiting for transfers between devices: 15.8 us -> none  [summed_on_arrival(): lax.all_to_all(in_blocks(array, dim, count), axis, 0, 0, tiled=True)]
    unnamed x6 -> x14, local copies, waits for them, and re-layouts: 0.02 us -> 8.61 us
    all_to_all x1 -> x0, starting transfers between devices: 8.3 us -> none  [summed_on_arrival(): lax.all_to_all(in_blocks(array, dim, count), axis, 0, 0, tiled=True)]
    reduce_sum x2 -> x0, other arithmetic: 3.09 us -> none  [summed_on_arrival(): return jnp.sum(blocks, axis=0)]
  transfers between devices with their start and end apart: 2 -> 0, of which waited for: 2 -> 0; matrix products, arithmetic and copies ran while one was open for 5% -> 0% of each run, Pallas kernels for 0% -> 0%
where the time goes in v1:
time: 70 us; the launch traced here: 69.5 us
  Pallas kernels  60.2 us (86%)
  local copies, waits for them, and re-layouts  8.61 us (12%)
    pallas_call x1, Pallas kernels, per_device(): pl.pallas_call(kernel, out_shape=(jax.ShapeDtypeStruct((8, DL), F32), jax...  60.2 us
    unnamed x14, local copies, waits for them, and re-layouts  8.61 us

profile of v1, /device:TPU:1, one launch (start us, length us, event | category | flops | bytes accessed | tf_op | source)
XLA Modules:
  0.0 69.5 jit_solution(8433521908405976563)
XLA Ops:
  0.6 0.0 copy-start
  0.6 1.2 %copy-done = f32[672,336]{1,0:T(8,128)S(1)} copy-done((f32[672,336]{1,0:T(8,128)S(1)}, f32[672,336]{1,0:T(8,128)}, u32[]{:S(2)}) %copy-start) | copy-done | bytes 903192
  1.9 0.0 copy-start.1
  1.9 1.2 %copy-done.1 = f32[672,336]{1,0:T(8,128)S(1)} copy-done((f32[672,336]{1,0:T(8,128)S(1)}, f32[672,336]{1,0:T(8,128)}, u32[]{:S(2)}) %copy-start.1) | copy-done | bytes 903192
  3.1 0.0 copy-start.2
  3.1 1.2 %copy-done.2 = f32[336,672]{1,0:T(8,128)S(1)} copy-done((f32[336,672]{1,0:T(8,128)S(1)}, f32[336,672]{1,0:T(8,128)}, u32[]{:S(2)}) %copy-start.2) | copy-done | bytes 903192
  4.3 0.0 copy-start.3
  4.3 0.7 %copy-done.3 = f32[8,672]{1,0:T(8,128)S(1)} copy-done((f32[8,672]{1,0:T(8,128)S(1)}, f32[8,672]{1,0:T(8,128)}, u32[]{:S(2)}) %copy-start.3) | copy-done | bytes 21528
  5.0 0.0 copy-start.4
  5.0 0.7 %copy-done.4 = f32[8,672]{1,0:T(8,128)S(1)} copy-done((f32[8,672]{1,0:T(8,128)S(1)}, f32[8,672]{1,0:T(8,128)}, u32[]{:S(2)}) %copy-start.4) | copy-done | bytes 21528
  5.8 60.2 %feed_forward_backward.1 = (f32[8,672]{1,0:T(8,128)S(1)}, f32[672,336]{1,0:T(8,128)S(1)}, f32[672,336]{1,0:T(8,128)S(1)}, f32[336,672]{1,0:T(8,128)S(1)}) custom-call(f32[8,672]{1,0:T(8,128)S(1)} %copy-done.3, f32[8,672]{1,0:T(8,128)S(1)} %copy-done.4, f32[672,336]{1,0:T(8,128)S(1)} %copy-done, f32[672,336]{1,0:T(8,128)S(1)} %copy-done.1, ...), custom_call_target="tpu_custom_call" | custom-call | tf_op jit(solution)/shard_map/feed_forward_backward/pallas_call | solution.py:261
  66.0 0.6 copy.13
  66.6 1.0 %copy.14 = f32[672,336]{1,0:T(8,128)} copy(f32[672,336]{1,0:T(8,128)S(1)} %get-tuple-element.9) | data formatting | bytes 1806336
  67.6 1.0 %copy.15 = f32[672,336]{1,0:T(8,128)} copy(f32[672,336]{1,0:T(8,128)S(1)} %get-tuple-element.10) | data formatting | bytes 1806336
  68.5 1.0 %copy.16 = f32[336,672]{1,0:T(8,128)} copy(f32[336,672]{1,0:T(8,128)S(1)} %get-tuple-element.11) | data formatting | bytes 1806336
Async XLA Ops:
  0.6 1.2 %copy-start = (f32[672,336]{1,0:T(8,128)S(1)}, f32[672,336]{1,0:T(8,128)}, u32[]{:S(2)}) copy-start(f32[672,336]{1,0:T(8,128)} %wg_hbm.1) | copy-start | bytes 2709508
  1.9 1.2 %copy-start.1 = (f32[672,336]{1,0:T(8,128)S(1)}, f32[672,336]{1,0:T(8,128)}, u32[]{:S(2)}) copy-start(f32[672,336]{1,0:T(8,128)} %wu_hbm.1) | copy-start | bytes 2709508
  3.1 1.2 %copy-start.2 = (f32[336,672]{1,0:T(8,128)S(1)}, f32[336,672]{1,0:T(8,128)}, u32[]{:S(2)}) copy-start(f32[336,672]{1,0:T(8,128)} %wd_hbm.1) | copy-start | bytes 2709508
  4.3 0.7 %copy-start.3 = (f32[8,672]{1,0:T(8,128)S(1)}, f32[8,672]{1,0:T(8,128)}, u32[]{:S(2)}) copy-start(f32[8,672]{1,0:T(8,128)} %tok.1) | copy-start | bytes 64516
  5.0 0.7 %copy-start.4 = (f32[8,672]{1,0:T(8,128)S(1)}, f32[8,672]{1,0:T(8,128)}, u32[]{:S(2)}) copy-start(f32[8,672]{1,0:T(8,128)} %gro.1) | copy-start | bytes 64516

commit v2 on v1

v2 whole, which is shorter than its diff:
```python
import jax
import jax.numpy as jnp
from jax import lax
from jax.experimental import pallas as pl
from jax.experimental.pallas import tpu as pltpu
from jax.sharding import PartitionSpec as P

MESH = pl.DeviceIdType.MESH
F32, BF16 = jnp.float32, jnp.bfloat16
DL, FL = 672, 336
DP, FP = 768, 384
XW, AW = 1408, 1024
STEPS = (0, 1, 2, 3)


def split(v):
    hi = v.astype(BF16)
    return hi, (v - hi.astype(F32)).astype(BF16)


def dot(a, b, ad, bd):
    return lax.dot_general(a, b, (((ad,), (bd,)), ((), ())), preferred_element_type=F32)


def pack3(a, b, c):
    rows = a.shape[0]
    return jnp.concatenate([a[:, :FL], b[:, :FL], c[:, :FL], jnp.zeros((rows, AW - 3 * FL), F32)], axis=1)


def unpack3(p):
    pad = jnp.zeros((p.shape[0], FP - FL), F32)
    return [jnp.concatenate([p[:, i * FL : (i + 1) * FL], pad], axis=1) for i in range(3)]


def derivs(gate, up, grad_hidden):
    sig = 1.0 / (1.0 + jnp.exp(-gate))
    hidden = gate * sig * up
    grad_up_act = grad_hidden * gate * sig
    grad_gate_act = grad_hidden * up * sig * (1.0 + gate * (1.0 - sig))
    return grad_gate_act, grad_up_act, hidden


def kernel(
    tok, gro, wg_hbm, wu_hbm, wd_hbm,
    o_tok, o_g, o_u, o_d,
    wg, wu, wd, wgu_h, wgu_l, wd_h, wd_l,
    x, xt_h, xt_l, xg_h, xg_l,
    part, part_in, acts, a_h, a_l,
    gb, gb_in, q, q_in, r, r_in,
    w_sem, az_s, az_r, ay_s, ay_r, as_s, as_r,
    b_s, b_r, c_s, c_r, d1_s, d1_r, d2_s, d2_r, d3_s, d3_r,
):
    wa, ha = lax.axis_index("wa"), lax.axis_index("ha")
    y, zh, c = ha // 8, (ha // 2) % 4, ha % 2

    def dev(w, yy, zz, cc):
        return (w, yy * 8 + zz * 2 + cc)

    sibling = dev(wa, y, zh, 1 - c)
    z_peers = [dev(wa, y, (zh + i) % 4, c) for i in (1, 2, 3)]
    y_peers = [dev(wa, (y + s) % 4, zh, c) for s in STEPS[1:]]
    w_peers = [dev((wa + i) % 8, y, zh, c) for i in range(1, 8)]

    loads = [
        pltpu.make_async_copy(wg_hbm, wg, w_sem.at[0]),
        pltpu.make_async_copy(wu_hbm, wu, w_sem.at[1]),
        pltpu.make_async_copy(wd_hbm, wd, w_sem.at[2]),
    ]
    for cp in loads:
        cp.start()

    barrier = pltpu.get_barrier_semaphore()
    for d in [sibling, *z_peers, *y_peers, *w_peers]:
        pl.semaphore_signal(barrier, inc=1, device_id=d, device_id_type=MESH)
    t, g = tok[...], gro[...]
    x[zh, c, y] = jnp.concatenate([t[:, :640], g[:, :640], t[:, 640:], g[:, 640:], jnp.zeros((8, 64), F32)], axis=1)
    pl.semaphore_wait(barrier, 14)

    sends = []

    def send(src, dst, ss, rs, d):
        cp = pltpu.make_async_remote_copy(src_ref=src, dst_ref=dst, send_sem=ss, recv_sem=rs, device_id=d, device_id_type=MESH)
        cp.start()
        sends.append(cp)

    def arrived(ref, sem):
        pltpu.make_async_copy(ref, ref, sem).wait()

    own = x.at[zh, c, y]
    for i in (0, 2, 1):
        send(own, own, ay_s.at[0, i], ay_r.at[0, i], y_peers[i])
    for i in (0, 2, 1):
        send(own, own, az_s.at[i], az_r.at[i], z_peers[i])

    wgu_h[DL:, :] = jnp.zeros((DP - DL, DP), BF16)
    wgu_l[DL:, :] = jnp.zeros((DP - DL, DP), BF16)
    wd_h[FL:, :] = jnp.zeros((FP - FL, DP), BF16)
    wd_l[FL:, :] = jnp.zeros((FP - FL, DP), BF16)
    loads[0].wait()
    loads[1].wait()

    @pl.loop(0, 7)
    def _(i):
        rows = pl.ds(pl.multiple_of(i * 96, 96), 96)
        pad = jnp.zeros((96, FP - FL), F32)
        hi, lo = split(jnp.concatenate([wg[rows, :], pad], axis=1))
        wgu_h[rows, :FP], wgu_l[rows, :FP] = hi, lo
        hi, lo = split(jnp.concatenate([wu[rows, :], pad], axis=1))
        wgu_h[rows, FP:], wgu_l[rows, FP:] = hi, lo

    loads[2].wait()

    @pl.loop(0, 7)
    def _(i):
        rows = pl.ds(pl.multiple_of(i * 48, 48), 48)
        hi, lo = split(jnp.concatenate([wd[rows, :], jnp.zeros((48, DP - DL), F32)], axis=1))
        wd_h[rows, :], wd_l[rows, :] = hi, lo

    def source_z(k):
        return (zh + 4 - STEPS[k]) % 4

    def pass_on(k):
        block = x.at[source_z(k), c, y]
        arrived(block, az_r.at[k - 1])
        for i in (0, 2, 1):
            send(block, block, ay_s.at[k, i], ay_r.at[k, i], y_peers[i])

    def forward(k):
        zz = source_z(k)
        for i in (0, 2, 1):
            arrived(x.at[zz, c, (y - i - 1 + 4) % 4], ay_r.at[k, i])
        send(x.at[zz, c], x.at[zz, c], as_s.at[k], as_r.at[k], sibling)

    lane = lax.broadcasted_iota(jnp.int32, (64, 128), 1)

    def project(k):
        zz = source_z(k)
        arrived(x.at[zz, 1 - c], as_r.at[k])
        rows = pl.ds(pl.multiple_of(zz * 64, 64), 64)
        v = x[zz].reshape(64, XW)
        mixed = v[:, 1280:]
        th, tl = split(jnp.concatenate([v[:, :640], jnp.where(lane < 32, mixed, 0.0)], axis=1))
        gh, gl = split(jnp.concatenate([v[:, 640:1280], jnp.where(lane < 32, pltpu.roll(mixed, 96, 1), 0.0)], axis=1))
        xt_h[rows, :], xt_l[rows, :] = th, tl
        xg_h[rows, :], xg_l[rows, :] = gh, gl
        both = jnp.concatenate([th, tl], axis=0)
        gu = dot(both, wgu_h[...], 1, 0)
        gu = gu[:64] + gu[64:] + dot(th, wgu_l[...], 1, 0)
        both = jnp.concatenate([gh, gl], axis=0)
        hid = dot(both, wd_h[...], 1, 1)
        hid = hid[:64] + hid[64:] + dot(gh, wd_l[...], 1, 1)
        part[k] = pack3(gu[:, :FP], gu[:, FP:], hid).reshape(8, 8, AW)
        for i in range(7):
            send(part.at[k, (wa + i + 1) % 8], part_in.at[k, i], b_s.at[k, i], b_r.at[k, i], w_peers[i])

    def activate(k):
        zz = source_z(k)
        total = part[k, wa]
        for i in range(7):
            arrived(part_in.at[k, i], b_r.at[k, i])
            total = total + part_in[k, i]
        gate, up, gh = unpack3(total)
        acts[zz, wa] = pack3(*derivs(gate, up, gh))
        mine = acts.at[zz, wa]
        for i in range(7):
            send(mine, mine, c_s.at[k, i], c_r.at[k, i], w_peers[i])

    def back(k):
        zz = source_z(k)
        for i in range(7):
            arrived(acts.at[zz, (wa - i - 1 + 8) % 8], c_r.at[k, i])
        rows = pl.ds(pl.multiple_of(zz * 64, 64), 64)
        gga, gua, hid = unpack3(acts[zz].reshape(64, AW))
        ah, al = split(jnp.concatenate([gga, gua], axis=1))
        hh, hl = split(hid)
        a_h[rows, :DP], a_l[rows, :DP] = ah, al
        a_h[rows, DP:], a_l[rows, DP:] = hh, hl
        both = jnp.concatenate([ah, al], axis=0)
        gt = dot(both, wgu_h[...], 1, 1)
        gt = gt[:64] + gt[64:] + dot(ah, wgu_l[...], 1, 1)
        gb[k] = gt.reshape(2, 4, 8, DP)
        send(gb.at[k, 1 - c], gb_in.at[k], d1_s.at[k], d1_r.at[k], sibling)

    def home(k):
        arrived(gb_in.at[k], d1_r.at[k])
        q[k] = gb[k, c] + gb_in[k]
        for i in (1, 0, 2):
            send(q.at[k, (y + i + 1) % 4], q_in.at[k, i], d2_s.at[k, i], d2_r.at[k, i], y_peers[i])

    def collect(k):
        total = q[k, y]
        for i in range(3):
            arrived(q_in.at[k, i], d2_r.at[k, i])
            total = total + q_in[k, i]
        r[k] = total
        if k:
            send(r.at[k], r_in.at[k - 1], d3_s.at[k - 1], d3_r.at[k - 1], dev(wa, y, source_z(k), c))

    def grad(lh, ll, rh, rl):
        return dot(lh, rh, 0, 0) + dot(lh, rl, 0, 0) + dot(ll, rh, 0, 0)

    forward(0)
    pass_on(1)
    pass_on(3)
    pass_on(2)
    project(0)
    forward(1)
    forward(3)
    project(1)
    project(3)
    forward(2)
    project(2)
    activate(1)
    activate(3)
    activate(2)
    activate(0)
    back(1)
    home(1)
    back(3)
    home(3)
    back(2)
    collect(1)
    home(2)
    collect(3)
    back(0)
    collect(2)
    home(0)
    gg = grad(xt_h[...], xt_l[...], a_h[:, :FP], a_l[:, :FP])
    o_g[...] = gg[:DL, :FL]
    gg = grad(xt_h[...], xt_l[...], a_h[:, FP:DP], a_l[:, FP:DP])
    o_u[...] = gg[:DL, :FL]
    collect(0)
    gg = grad(a_h[:, DP:], a_l[:, DP:], xg_h[...], xg_l[...])
    o_d[...] = gg[:FL, :DL]

    total = r[0]
    for i in range(3):
        arrived(r_in.at[i], d3_r.at[i])
        total = total + r_in[i]
    o_tok[...] = total[:, :DL]
    for cp in sends:
        cp.wait_send()


def write_out(*refs):
    sem = refs[-1]
    copies = [pltpu.make_async_copy(refs[i], refs[4 + i], sem.at[i]) for i in range(4)]
    for cp in copies:
        cp.start()
    for cp in copies:
        cp.wait()


def per_device(tokens, grad_out, gate_weight, up_weight, down_weight):
    vm, anym = pl.BlockSpec(memory_space=pltpu.VMEM), pl.BlockSpec(memory_space=pltpu.MemorySpace.HBM)
    dma = pltpu.SemaphoreType.DMA
    v = pltpu.VMEM
    shapes = tuple(jax.ShapeDtypeStruct(s, F32) for s in ((8, DL), (DL, FL), (DL, FL), (FL, DL)))
    hbm = pltpu.MemorySpace.HBM
    tokens, grad_out, gate_weight, up_weight, down_weight = (
        pltpu.with_memory_space_constraint(a, hbm) for a in (tokens, grad_out, gate_weight, up_weight, down_weight)
    )
    results = pl.pallas_call(
        kernel,
        out_shape=shapes,
        in_specs=[vm, vm, anym, anym, anym],
        out_specs=(vm,) * 4,
        scratch_shapes=[
            v((DL, FL), F32), v((DL, FL), F32), v((FL, DL), F32),
            v((DP, DP), BF16), v((DP, DP), BF16), v((FP, DP), BF16), v((FP, DP), BF16),
            v((4, 2, 4, 8, XW), F32),
            v((256, DP), BF16), v((256, DP), BF16), v((256, DP), BF16), v((256, DP), BF16),
            v((4, 8, 8, AW), F32), v((4, 7, 8, AW), F32), v((4, 8, 8, AW), F32),
            v((256, DP + FP), BF16), v((256, DP + FP), BF16),
            v((4, 2, 4, 8, DP), F32), v((4, 4, 8, DP), F32), v((4, 4, 8, DP), F32), v((4, 3, 8, DP), F32),
            v((4, 8, DP), F32), v((3, 8, DP), F32),
            dma((3,)), dma((3,)), dma((3,)), dma((4, 3)), dma((4, 3)), dma((4,)), dma((4,)),
            dma((4, 7)), dma((4, 7)), dma((4, 7)), dma((4, 7)),
            dma((4,)), dma((4,)), dma((4, 3)), dma((4, 3)), dma((3,)), dma((3,)),
        ],
        compiler_params=pltpu.CompilerParams(collective_id=0, has_side_effects=True, vmem_limit_bytes=40 * 2**20),
        name="feed_forward_backward",
    )(tokens, grad_out, gate_weight, up_weight, down_weight)
    return pl.pallas_call(
        write_out,
        out_shape=shapes,
        in_specs=[anym] * 4,
        out_specs=(anym,) * 4,
        scratch_shapes=[dma((4,))],
        compiler_params=pltpu.CompilerParams(vmem_limit_bytes=2**20),
        name="write_out",
    )(*results)


def solution(mesh):
    placed = (P("ha", "wa"), P("ha", "wa"), P("wa", "ha"), P("wa", "ha"), P("ha", "wa"))
    return jax.shard_map(
        per_device,
        mesh=mesh,
        in_specs=placed,
        out_specs=(P("ha", "wa"), P("wa", "ha"), P("wa", "ha"), P("ha", "wa")),
        check_vma=False,
    )
```

time: 70 us -> 57.5 us (0.82)
  local copies, waits for them, and re-layouts: 8.61 us -> 0 us
  Pallas kernels: 60.2 us -> 56.7 us
    unnamed x14 -> x0, local copies, waits for them, and re-layouts: 8.61 us -> none
    pallas_call x1 -> x2, Pallas kernels: 60.2 us -> 56.7 us  [the longest x1 55 us: per_device(): pl.pallas_call(kernel, out_shape=shapes, in_specs=[vm, vm, anym, anym, an...]
where the time goes in v2:
time: 57.5 us; the launch traced here: 57.3 us
  Pallas kernels  56.7 us (99%)
  between operations  0.64 us (1%)
    pallas_call x1, Pallas kernels, per_device(): pl.pallas_call(kernel, out_shape=shapes, in_specs=[vm, vm, anym, anym, an...  55 us
    pallas_call x1, Pallas kernels, per_device(): pl.pallas_call(write_out, out_shape=shapes, in_specs=[anym] * 4, out_spec...  1.69 us

profile of v2, /device:TPU:1, one launch (start us, length us, event | category | flops | bytes accessed | tf_op | source)
XLA Modules:
  0.0 57.3 jit_solution(498731638000140627)
XLA Ops:
  0.6 55.0 %feed_forward_backward.1 = (f32[8,672]{1,0:T(8,128)S(1)}, f32[672,336]{1,0:T(8,128)S(1)}, f32[672,336]{1,0:T(8,128)S(1)}, f32[336,672]{1,0:T(8,128)S(1)}) custom-call(f32[8,672]{1,0:T(8,128)} %tok.1, f32[8,672]{1,0:T(8,128)} %gro.1, f32[672,336]{1,0:T(8,128)} %wg_hbm.1, f32[672,336]{1,0:T(8,128)} %wu_hbm.1, f32[336,672]{1,0:T(8,128)} %wd_hbm.1), custom_call_target="tpu_custom_call" | custom-call | tf_op jit(solution)/shard_map/feed_forward_backward/pallas_call | solution.py:263
  55.6 1.7 %write_out.1 = (f32[8,672]{1,0:T(8,128)}, f32[672,336]{1,0:T(8,128)}, f32[672,336]{1,0:T(8,128)}, f32[336,672]{1,0:T(8,128)}) custom-call(f32[8,672]{1,0:T(8,128)S(1)} %get-tuple-element.8.refs_0_, f32[672,336]{1,0:T(8,128)S(1)} %get-tuple-element.9.refs_1_, f32[672,336]{1,0:T(8,128)S(1)} %get-tuple-element.10.refs_2_, f32[336,672]{1,0:T(8,128)S(1)} %get-tuple-element.11.refs_3_), custom_call_target="tpu_custom_call" | custom-call | tf_op jit(solution)/shard_map/write_out/pallas_call | solution.py:284

commit v3 on v2

--- a/solution.py
+++ b/solution.py
@@ -11,6 +11,8 @@
 DP, FP = 768, 384
 XW, AW = 1408, 1024
 STEPS = (0, 1, 2, 3)
+STAGED = (0,)
+FAR_FIRST = (1, 0, 2)
 
 
 def split(v):
@@ -41,11 +43,11 @@
 
 
 def kernel(
-    tok, gro, wg_hbm, wu_hbm, wd_hbm,
+    tok_hbm, gro_hbm, wg_hbm, wu_hbm, wd_hbm,
     o_tok, o_g, o_u, o_d,
-    wg, wu, wd, wgu_h, wgu_l, wd_h, wd_l,
+    tok, gro, wg, wu, wd, wgu_h, wgu_l, wd_h, wd_l,
     x, xt_h, xt_l, xg_h, xg_l,
-    part, part_in, acts, a_h, a_l,
+    part, near, far, right, right_in, right2_in, acts, a_h, a_l,
     gb, gb_in, q, q_in, r, r_in,
     w_sem, az_s, az_r, ay_s, ay_r, as_s, as_r,
     b_s, b_r, c_s, c_r, d1_s, d1_r, d2_s, d2_r, d3_s, d3_r,
@@ -59,21 +61,32 @@
     sibling = dev(wa, y, zh, 1 - c)
     z_peers = [dev(wa, y, (zh + i) % 4, c) for i in (1, 2, 3)]
     y_peers = [dev(wa, (y + s) % 4, zh, c) for s in STEPS[1:]]
-    w_peers = [dev((wa + i) % 8, y, zh, c) for i in range(1, 8)]
-
+    zl, xx = wa // 4, wa % 4
+    partner = dev((1 - zl) * 4 + xx, y, zh, c)
+    x_peers = [dev(zl * 4 + (xx + i) % 4, y, zh, c) for i in (1, 2, 3)]
+    cross = [((xx + i) % 4, dev((1 - zl) * 4 + (xx + i) % 4, y, zh, c)) for i in (1, 2, 3)]
+
+    first = [
+        pltpu.make_async_copy(tok_hbm, tok, w_sem.at[3]),
+        pltpu.make_async_copy(gro_hbm, gro, w_sem.at[4]),
+    ]
     loads = [
         pltpu.make_async_copy(wg_hbm, wg, w_sem.at[0]),
         pltpu.make_async_copy(wu_hbm, wu, w_sem.at[1]),
         pltpu.make_async_copy(wd_hbm, wd, w_sem.at[2]),
     ]
+    for cp in first:
+        cp.start()
+
+    barrier = pltpu.get_barrier_semaphore()
+    for d in [sibling, *z_peers, *y_peers, partner, *x_peers, *[d for _, d in cross]]:
+        pl.semaphore_signal(barrier, inc=1, device_id=d, device_id_type=MESH)
+    first[0].wait()
+    first[1].wait()
+    t, g = tok[...], gro[...]
+    x[zh, c, y] = jnp.concatenate([t[:, :640], g[:, :640], t[:, 640:], g[:, 640:], jnp.zeros((8, 64), F32)], axis=1)
     for cp in loads:
         cp.start()
-
-    barrier = pltpu.get_barrier_semaphore()
-    for d in [sibling, *z_peers, *y_peers, *w_peers]:
-        pl.semaphore_signal(barrier, inc=1, device_id=d, device_id_type=MESH)
-    t, g = tok[...], gro[...]
-    x[zh, c, y] = jnp.concatenate([t[:, :640], g[:, :640], t[:, 640:], g[:, 640:], jnp.zeros((8, 64), F32)], axis=1)
     pl.semaphore_wait(barrier, 14)
 
     sends = []
@@ -87,7 +100,7 @@
         pltpu.make_async_copy(ref, ref, sem).wait()
 
     own = x.at[zh, c, y]
-    for i in (0, 2, 1):
+    for i in FAR_FIRST:
         send(own, own, ay_s.at[0, i], ay_r.at[0, i], y_peers[i])
     for i in (0, 2, 1):
         send(own, own, az_s.at[i], az_r.at[i], z_peers[i])
@@ -122,7 +135,7 @@
     def pass_on(k):
         block = x.at[source_z(k), c, y]
         arrived(block, az_r.at[k - 1])
-        for i in (0, 2, 1):
+        for i in FAR_FIRST:
             send(block, block, ay_s.at[k, i], ay_r.at[k, i], y_peers[i])
 
     def forward(k):
@@ -149,26 +162,54 @@
         both = jnp.concatenate([gh, gl], axis=0)
         hid = dot(both, wd_h[...], 1, 1)
         hid = hid[:64] + hid[64:] + dot(gh, wd_l[...], 1, 1)
-        part[k] = pack3(gu[:, :FP], gu[:, FP:], hid).reshape(8, 8, AW)
-        for i in range(7):
-            send(part.at[k, (wa + i + 1) % 8], part_in.at[k, i], b_s.at[k, i], b_r.at[k, i], w_peers[i])
+        part[k] = pack3(gu[:, :FP], gu[:, FP:], hid).reshape(4, 2, 8, AW)
+        if k not in STAGED:
+            for i in FAR_FIRST:
+                send(part.at[k, cross[i][0], 1 - zl], far.at[k, i], b_s.at[k, 4 + i], b_r.at[k, 4 + i], cross[i][1])
+            for i in FAR_FIRST:
+                send(part.at[k, (xx + i + 1) % 4, zl], near.at[k, i], b_s.at[k, i], b_r.at[k, i], x_peers[i])
+            send(part.at[k, xx, 1 - zl], far.at[k, 3], b_s.at[k, 3], b_r.at[k, 3], partner)
+        else:
+            for i in range(3):
+                send(part.at[k, (xx + i + 1) % 4], right_in.at[k, i], b_s.at[k, i], b_r.at[k, i], x_peers[i])
+
+    def reduce(k):
+        total = part[k, xx]
+        for i in range(3):
+            arrived(right_in.at[k, i], b_r.at[k, i])
+            total = total + right_in[k, i]
+        right[k] = total
+        send(right.at[k, 1 - zl], right2_in.at[k], b_s.at[k, 7], b_r.at[k, 7], partner)
 
     def activate(k):
         zz = source_z(k)
-        total = part[k, wa]
-        for i in range(7):
-            arrived(part_in.at[k, i], b_r.at[k, i])
-            total = total + part_in[k, i]
+        if k not in STAGED:
+            total = part[k, xx, zl]
+            for i in range(3):
+                arrived(near.at[k, i], b_r.at[k, i])
+                total = total + near[k, i]
+            for i in (3, 0, 1, 2):
+                arrived(far.at[k, i], b_r.at[k, 3 if i == 3 else 4 + i])
+                total = total + far[k, i]
+        else:
+            arrived(right2_in.at[k], b_r.at[k, 7])
+            total = right[k, zl] + right2_in[k]
         gate, up, gh = unpack3(total)
-        acts[zz, wa] = pack3(*derivs(gate, up, gh))
-        mine = acts.at[zz, wa]
-        for i in range(7):
-            send(mine, mine, c_s.at[k, i], c_r.at[k, i], w_peers[i])
+        acts[zz, xx, zl] = pack3(*derivs(gate, up, gh))
+        mine = acts.at[zz, xx, zl]
+        for i in FAR_FIRST:
+            send(mine, mine, c_s.at[k, 4 + i], c_r.at[k, 4 + i], cross[i][1])
+        for i in FAR_FIRST:
+            send(mine, mine, c_s.at[k, i], c_r.at[k, i], x_peers[i])
+        send(mine, mine, c_s.at[k, 3], c_r.at[k, 3], partner)
 
     def back(k):
         zz = source_z(k)
-        for i in range(7):
-            arrived(acts.at[zz, (wa - i - 1 + 8) % 8], c_r.at[k, i])
+        for i in range(3):
+            x2 = (xx - i - 1 + 4) % 4
+            arrived(acts.at[zz, x2, zl], c_r.at[k, i])
+            arrived(acts.at[zz, x2, 1 - zl], c_r.at[k, 4 + i])
+        arrived(acts.at[zz, xx, 1 - zl], c_r.at[k, 3])
         rows = pl.ds(pl.multiple_of(zz * 64, 64), 64)
         gga, gua, hid = unpack3(acts[zz].reshape(64, AW))
         ah, al = split(jnp.concatenate([gga, gua], axis=1))
@@ -210,21 +251,22 @@
     project(3)
     forward(2)
     project(2)
+    reduce(0)
     activate(1)
+    activate(2)
     activate(3)
-    activate(2)
     activate(0)
     back(1)
     home(1)
+    back(2)
+    home(2)
+    collect(1)
     back(3)
     home(3)
-    back(2)
-    collect(1)
-    home(2)
+    collect(2)
+    back(0)
+    home(0)
     collect(3)
-    back(0)
-    collect(2)
-    home(0)
     gg = grad(xt_h[...], xt_l[...], a_h[:, :FP], a_l[:, :FP])
     o_g[...] = gg[:DL, :FL]
     gg = grad(xt_h[...], xt_l[...], a_h[:, FP:DP], a_l[:, FP:DP])
@@ -263,19 +305,21 @@
     results = pl.pallas_call(
         kernel,
         out_shape=shapes,
-        in_specs=[vm, vm, anym, anym, anym],
+        in_specs=[anym] * 5,
         out_specs=(vm,) * 4,
         scratch_shapes=[
-            v((DL, FL), F32), v((DL, FL), F32), v((FL, DL), F32),
+            v((8, DL), F32), v((8, DL), F32), v((DL, FL), F32), v((DL, FL), F32), v((FL, DL), F32),
             v((DP, DP), BF16), v((DP, DP), BF16), v((FP, DP), BF16), v((FP, DP), BF16),
             v((4, 2, 4, 8, XW), F32),
             v((256, DP), BF16), v((256, DP), BF16), v((256, DP), BF16), v((256, DP), BF16),
-            v((4, 8, 8, AW), F32), v((4, 7, 8, AW), F32), v((4, 8, 8, AW), F32),
+            v((4, 4, 2, 8, AW), F32), v((4, 3, 8, AW), F32), v((4, 4, 8, AW), F32),
+            v((4, 2, 8, AW), F32), v((4, 3, 2, 8, AW), F32), v((4, 8, AW), F32),
+            v((4, 4, 2, 8, AW), F32),
             v((256, DP + FP), BF16), v((256, DP + FP), BF16),
             v((4, 2, 4, 8, DP), F32), v((4, 4, 8, DP), F32), v((4, 4, 8, DP), F32), v((4, 3, 8, DP), F32),
             v((4, 8, DP), F32), v((3, 8, DP), F32),
-            dma((3,)), dma((3,)), dma((3,)), dma((4, 3)), dma((4, 3)), dma((4,)), dma((4,)),
-            dma((4, 7)), dma((4, 7)), dma((4, 7)), dma((4, 7)),
+            dma((5,)), dma((3,)), dma((3,)), dma((4, 3)), dma((4, 3)), dma((4,)), dma((4,)),
+            dma((4, 8)), dma((4, 8)), dma((4, 8)), dma((4, 8)),
             dma((4,)), dma((4,)), dma((4, 3)), dma((4, 3)), dma((3,)), dma((3,)),
         ],
         compiler_params=pltpu.CompilerParams(collective_id=0, has_side_effects=True, vmem_limit_bytes=40 * 2**20),

time: 57.5 us -> 55.7 us (0.969)
  Pallas kernels: 56.7 us -> 54.9 us
    pallas_call x1, Pallas kernels: 55 us -> 53.2 us  [per_device(): pl.pallas_call(kernel, out_shape=shapes, in_specs=[anym] * 5, out_specs=(...]
where the time goes in v3:
time: 55.7 us; the launch traced here: 55.5 us
  Pallas kernels  54.9 us (99%)
  between operations  0.64 us (1%)
    pallas_call x1, Pallas kernels, per_device(): pl.pallas_call(kernel, out_shape=shapes, in_specs=[anym] * 5, out_specs=(...  53.2 us
    pallas_call x1, Pallas kernels, per_device(): pl.pallas_call(write_out, out_shape=shapes, in_specs=[anym] * 4, out_spec...  1.69 us

profile of v3, /device:TPU:1, one launch (start us, length us, event | category | flops | bytes accessed | tf_op | source)
XLA Modules:
  0.0 55.5 jit_solution(12225844861706220738)
XLA Ops:
  0.6 53.2 %feed_forward_backward.1 = (f32[8,672]{1,0:T(8,128)S(1)}, f32[672,336]{1,0:T(8,128)S(1)}, f32[672,336]{1,0:T(8,128)S(1)}, f32[336,672]{1,0:T(8,128)S(1)}) custom-call(f32[8,672]{1,0:T(8,128)} %tok_hbm.1, f32[8,672]{1,0:T(8,128)} %gro_hbm.1, f32[672,336]{1,0:T(8,128)} %wg_hbm.1, f32[672,336]{1,0:T(8,128)} %wu_hbm.1, f32[336,672]{1,0:T(8,128)} %wd_hbm.1), custom_call_target="tpu_custom_call" | custom-call | tf_op jit(solution)/shard_map/feed_forward_backward/pallas_call | solution.py:305
  53.8 1.7 %write_out.1 = (f32[8,672]{1,0:T(8,128)}, f32[672,336]{1,0:T(8,128)}, f32[672,336]{1,0:T(8,128)}, f32[336,672]{1,0:T(8,128)}) custom-call(f32[8,672]{1,0:T(8,128)S(1)} %get-tuple-element.8.refs_0_, f32[672,336]{1,0:T(8,128)S(1)} %get-tuple-element.9.refs_1_, f32[672,336]{1,0:T(8,128)S(1)} %get-tuple-element.10.refs_2_, f32[336,672]{1,0:T(8,128)S(1)} %get-tuple-element.11.refs_3_), custom_call_target="tpu_custom_call" | custom-call | tf_op jit(solution)/shard_map/write_out/pallas_call | solution.py:328

commit v4 on v3

--- a/solution.py
+++ b/solution.py
@@ -275,13 +275,13 @@
     gg = grad(a_h[:, DP:], a_l[:, DP:], xg_h[...], xg_l[...])
     o_d[...] = gg[:FL, :DL]
 
+    for cp in sends:
+        cp.wait_send()
     total = r[0]
     for i in range(3):
         arrived(r_in.at[i], d3_r.at[i])
         total = total + r_in[i]
     o_tok[...] = total[:, :DL]
-    for cp in sends:
-        cp.wait_send()
 
 
 def write_out(*refs):

time: 55.7 us -> 55.5 us (level)
  no operation moved by 1% of the time
where the time goes in v4:
time: 55.5 us; the launch traced here: 55.3 us
  Pallas kernels  54.7 us (99%)
  between operations  0.64 us (1%)
    pallas_call x1, Pallas kernels, per_device(): pl.pallas_call(kernel, out_shape=shapes, in_specs=[anym] * 5, out_specs=(...  53 us
    pallas_call x1, Pallas kernels, per_device(): pl.pallas_call(write_out, out_shape=shapes, in_specs=[anym] * 4, out_spec...  1.69 us

profile of v4, /device:TPU:1, one launch (start us, length us, event | category | flops | bytes accessed | tf_op | source)
XLA Modules:
  0.0 55.3 jit_solution(18075627955938929582)
XLA Ops:
  0.6 53.0 %feed_forward_backward.1 = (f32[8,672]{1,0:T(8,128)S(1)}, f32[672,336]{1,0:T(8,128)S(1)}, f32[672,336]{1,0:T(8,128)S(1)}, f32[336,672]{1,0:T(8,128)S(1)}) custom-call(f32[8,672]{1,0:T(8,128)} %tok_hbm.1, f32[8,672]{1,0:T(8,128)} %gro_hbm.1, f32[672,336]{1,0:T(8,128)} %wg_hbm.1, f32[672,336]{1,0:T(8,128)} %wu_hbm.1, f32[336,672]{1,0:T(8,128)} %wd_hbm.1), custom_call_target="tpu_custom_call" | custom-call | tf_op jit(solution)/shard_map/feed_forward_backward/pallas_call | solution.py:305
  53.7 1.7 %write_out.1 = (f32[8,672]{1,0:T(8,128)}, f32[672,336]{1,0:T(8,128)}, f32[672,336]{1,0:T(8,128)}, f32[336,672]{1,0:T(8,128)}) custom-call(f32[8,672]{1,0:T(8,128)S(1)} %get-tuple-element.8.refs_0_, f32[672,336]{1,0:T(8,128)S(1)} %get-tuple-element.9.refs_1_, f32[672,336]{1,0:T(8,128)S(1)} %get-tuple-element.10.refs_2_, f32[336,672]{1,0:T(8,128)S(1)} %get-tuple-element.11.refs_3_), custom_call_target="tpu_custom_call" | custom-call | tf_op jit(solution)/shard_map/write_out/pallas_call | solution.py:328
